TPU v7x, 32 devices: a whole 2x2x4 slice. The times are simulated.
32 devices in a mesh: tm: 16 (over z, x, core), freq: 2 (over y).
Axes of the slice: x: 2, y: 2, z: 4, core: 2. Of those that a mesh axis runs over, the one named last changes fastest.
Arguments:
- visibilities: float32 [16, 2, 8, 512], P('tm', 'freq'), may hold values from -6 to 6
- coherency: bfloat16 [16, 2, 8, 64, 512], P('tm', 'freq'), may hold values from -0.75 to 0.75
- stations: int32 [16, 2, 512], P('tm'), may hold values from 0 to 511, as said below
- jones: float32 [2, 8, 32768], P('freq', None, 'tm'), may hold values from -3 to 3
- dual: float32 [2, 8, 32768], P('freq', None, 'tm'), may hold values from -1.8 to 1.8
- cluster: int32 [64], replicated, may hold values from 0 to 7
- rho_table: float32 [8], replicated, may hold values from 0.3 to 3
Outputs:
- jones_out: float32 [2, 8, 32768], P('freq', None, 'tm')
- dual_out: float32 [2, 8, 32768], P('freq', None, 'tm')
- consensus: float32 [1, 8, 32768], P(None, None, 'tm')
Inputs may be any that keep to these rules, and one draw needn't show every extreme that they name: Each baseline joins two different stations.
All inputs are finite; a program needn't handle non-finite values.
Results may differ from a plain program's by a relative error of at most 0.0003.
Values may be sent and summed in bfloat16 or wider, within the bound.
A program may use at most 64 MiB of HBM per device.

v0:
```python
import functools
import math

import jax
import jax.numpy as jnp
import numpy as np
from jax import lax
from jax.experimental import pallas as pl
from jax.experimental.pallas import tpu as pltpu
from jax.sharding import PartitionSpec as P

ITERS = 2
MESH = pl.DeviceIdType.MESH
ROWS = 8

step_size = 0.5
epsilon = 1e-06


def poly_basis(channels, degrees):
    points = np.linspace(-1.0, 1.0, channels)
    columns = []
    for degree in range(degrees):
        column = points**degree
        for earlier in columns:
            column = column - np.dot(earlier, column) * earlier
        column = column / np.sqrt(np.dot(column, column))
        columns.append(column)
    return np.stack(columns, axis=1).astype(np.float32)


def split_entries(parts):
    return [[(parts[4 * i + 2 * j], parts[4 * i + 2 * j + 1]) for j in range(2)] for i in range(2)]


def join_entries(mat):
    return [part for row in mat for entry in row for part in entry]


def times_pair(a, b):
    return (a[0] * b[0] - a[1] * b[1], a[0] * b[1] + a[1] * b[0])


def times_conj(a, b):
    return (a[0] * b[0] + a[1] * b[1], a[1] * b[0] - a[0] * b[1])


def add_pairs(a, b):
    return (a[0] + b[0], a[1] + b[1])


def mat_mul(a, b):
    return [[add_pairs(times_pair(a[i][0], b[0][j]), times_pair(a[i][1], b[1][j])) for j in range(2)] for i in range(2)]


def mat_mul_right_h(a, b):
    return [[add_pairs(times_conj(a[i][0], b[j][0]), times_conj(a[i][1], b[j][1])) for j in range(2)] for i in range(2)]


def mat_mul_left_h(a, b):
    return [[add_pairs(times_conj(b[0][j], a[0][i]), times_conj(b[1][j], a[1][i])) for j in range(2)] for i in range(2)]


def kernel(
    T, F, Z, nd, S, K, N, basis, weight,
    vis_hbm, coh_hbm, st_hbm, jones_hbm, dual_hbm, cluster_ref, table_ref,
    jones_out, dual_out, poly_out,
    vis_all, coh_raw, coh_out, coh_in, st_all, oh, tab, tabs, gz, zde, gp, abuf, xbuf, partial, part_in, res, acc, gout, gin,
    jn, du, de, fit, rho, sq, sqs,
    raw_sem, vi_ss, vi_rs, st_ss, st_rs, coh_ss, coh_rs, gz_ss, gz_rs, zd_ss, zd_rs, pa_ss, pa_rs, go_ss, go_rs,
    in_ss, in_rs, de_ss, de_rs, sq_ss, sq_rs, ss_ss, ss_rs,
):
    me = lax.axis_index("tm")
    fi = lax.axis_index("freq")
    Q = T // Z
    z, q = me // Q, lax.rem(me, Q)
    D = Z * nd
    tiles = D // ROWS
    g = ROWS // nd
    L = nd * S
    lane_tiles = S // 128
    half = S // 2
    degrees = basis.shape[1]

    def remote(src, dst, send, recv, to):
        return pltpu.make_async_remote_copy(
            src_ref=src, dst_ref=dst, send_sem=send, recv_sem=recv, device_id=to, device_id_type=MESH)

    def plane(u):
        return {"tm": z * Q + u}

    def column(v):
        return {"tm": v * Q + q}

    def st_copy(src, to):
        return remote(st_all.at[src], st_all.at[src], st_ss.at[to], st_rs.at[src], plane(to))

    def coh_copy(src, to):
        return remote(coh_out.at[to], coh_in.at[src], coh_ss.at[to], coh_rs.at[src], plane(to))

    def vis_copy(src, to):
        return remote(vis_all.at[src], vis_all.at[src], vi_ss.at[to], vi_rs.at[src], plane(to))

    def part_copy(it, u, src, to):
        return remote(
            partial.at[it, u], part_in.at[it, u, src], pa_ss.at[it, u, to], pa_rs.at[it, u, src], plane(to))

    def gz_copy(src, to):
        return remote(gz.at[src], gz.at[src], gz_ss.at[to], gz_rs.at[src], column(to))

    def zd_copy(it, src, to):
        return remote(de.at[it, fi], zde.at[it, src], zd_ss.at[it, to], zd_rs.at[it, src], column(to))

    def go_copy(it, h, src, to):
        return remote(gout.at[it, h, to], gin.at[it, h, src], go_ss.at[it, h, to], go_rs.at[it, h, src], column(to))

    def state_copy(which, src, to):
        ref = (jn, du)[which]
        return remote(ref.at[src], ref.at[src], in_ss.at[which, to], in_rs.at[which, src], {"freq": to})

    def de_copy(it, src, to):
        return remote(de.at[it, src], de.at[it, src], de_ss.at[it, to], de_rs.at[it, src], {"freq": to})

    def sq_copy(it, to):
        return remote(sq.at[it, q], sq.at[it, q], sq_ss.at[it], sq_rs.at[it], plane(to))

    def sq_all(it):
        span = sq.at[it, pl.ds(0, Q - 1)]
        return remote(span, span, sq_ss.at[it], sq_rs.at[it], plane(q))

    def sums_copy(it, to_f, to_v):
        mine = fi * Z + z
        return remote(
            sqs.at[it, mine], sqs.at[it, mine], ss_ss.at[it], ss_rs.at[it], {"tm": to_v * Q + q, "freq": to_f})

    def sums_all(it):
        span = sqs.at[it, pl.ds(0, F * Z - 1)]
        return remote(span, span, ss_ss.at[it], ss_rs.at[it], {"tm": me, "freq": fi})

    def each_other(fn):
        def one(o, _):
            other = lax.rem(fi * Z + z + o, F * Z)
            fn(other // Z, lax.rem(other, Z))
            return 0
        lax.fori_loop(1, F * Z, one, 0)

    plane_next = [lax.rem(q + o, Q) for o in range(1, Q)]
    plane_from = [lax.rem(q - o + Q, Q) for o in range(1, Q)]
    column_others = [lax.rem(z + o, Z) for o in range(1, Z)]
    freq_others = [lax.rem(fi + o, F) for o in range(1, F)]

    jones_in = pltpu.make_async_copy(jones_hbm, jn.at[fi], raw_sem.at[0])
    st_in = pltpu.make_async_copy(st_hbm, st_all.at[q], raw_sem.at[1])
    raw = pltpu.make_async_copy(coh_hbm, coh_raw, raw_sem.at[2])
    dual_in = pltpu.make_async_copy(dual_hbm, du.at[fi], raw_sem.at[3])
    vis_in = pltpu.make_async_copy(vis_hbm, vis_all.at[q], raw_sem.at[4])
    for copy in (jones_in, st_in, raw, dual_in, vis_in):
        copy.start()
    barrier = pltpu.get_barrier_semaphore()

    for u in plane_next:
        pl.semaphore_signal(barrier, inc=1, device_id=plane(u), device_id_type=MESH)
    each_other(lambda f, v: pl.semaphore_signal(
        barrier, inc=1, device_id={"tm": v * Q + q, "freq": f}, device_id_type=MESH))
    jones_in.wait()
    gz[z] = jn[fi]
    st_in.wait()
    for d in range(nd):
        value = table_ref[cluster_ref[me * nd + d]]
        rho[:, d * S:(d + 1) * S] = jnp.full((ROWS, S), value, jnp.float32)
    pl.semaphore_wait(barrier, Q - 1 + F * Z - 1)

    for to in plane_next:
        st_copy(q, to).start()
    for to in column_others:
        gz_copy(z, to).start()
    raw.wait()

    slot = lax.broadcasted_iota(jnp.int32, (ROWS, N), 0) // nd
    for c in range(8):
        full = coh_raw[c].astype(jnp.float32)
        for u in range(Q):
            rows = []
            for m in range(tiles):
                out = None
                for s in range(g):
                    unit = (m * g + s) * Q + u
                    tile = full[8 * (unit // g):8 * (unit // g) + 8, :]
                    shift = ((s - unit % g) % g) * nd
                    if shift:
                        tile = pltpu.roll(tile, shift, 0)
                    out = tile if s == 0 else jnp.where(slot == s, tile, out)
                rows.append(out)
            block = rows[0] if tiles == 1 else jnp.concatenate(rows, axis=0)
            coh_out[u, c * D:(c + 1) * D, :] = block.astype(jnp.bfloat16)
    for to in plane_next:
        coh_copy(q, to).start()
    coh_in[q] = coh_out[q]
    dual_in.wait()
    vis_in.wait()
    for to in plane_next:
        vis_copy(q, to).start()
    for to in freq_others:
        state_copy(0, fi, to).start()
        state_copy(1, fi, to).start()

    def build(i, _):
        u = lax.rem(q - i + Q, Q)

        @pl.when(u != q)
        def _():
            st_copy(u, q).wait_recv()
        for e in range(2):
            row = st_all[u, e:e + 1, :]
            for lo in range(0, S, 64):
                ids = lax.broadcasted_iota(jnp.int32, (64, N), 0) + lo
                oh[u, lo:lo + 64, e * N:(e + 1) * N] = jnp.where(ids == row, 1.0, 0.0).astype(jnp.bfloat16)
        return 0

    lax.fori_loop(0, Q, build, 0)

    def set_table():
        for v in range(Z):
            now = gz[v]
            for d in range(nd):
                piece = now[:, d * S:(d + 1) * S]
                high = piece.astype(jnp.bfloat16).astype(jnp.float32)
                low = piece - high
                for k in range(lane_tiles):
                    lanes = slice(k * 128, (k + 1) * 128)
                    tabs[0, k, pl.ds(v * nd + d, 8, stride=D), :] = high[:, lanes]
                    tabs[1, k, pl.ds(v * nd + d, 8, stride=D), :] = low[:, lanes]
        for h in range(2):
            for k in range(lane_tiles):
                tab[h * 8 * D:(h + 1) * 8 * D, k * 128:(k + 1) * 128] = tabs[h, k].astype(jnp.bfloat16)

    def gather_time(u):
        for e in range(2):
            got = jnp.dot(tab[...], oh[u, :, e * N:(e + 1) * N], preferred_element_type=jnp.float32)
            gp[u, e] = got[:8 * D] + got[8 * D:]

    def tile_rows(c, m):
        return slice(c * D + m * ROWS, c * D + (m + 1) * ROWS)

    def sky_tiles(u, lanes):
        sky = [coh_in[u, c * D:(c + 1) * D, lanes].astype(jnp.float32) for c in range(8)]
        return [split_entries([part[m * ROWS:(m + 1) * ROWS] for part in sky]) for m in range(tiles)]

    def forward_time(it, u):
        for lo in range(0, N, 128):
            lanes = slice(lo, lo + 128)
            sky = sky_tiles(u, lanes)
            sums = None
            for m in range(tiles):
                first = split_entries([gp[u, 0, tile_rows(c, m), lanes] for c in range(8)])
                second = split_entries([gp[u, 1, tile_rows(c, m), lanes] for c in range(8)])
                prod = mat_mul(first, sky[m])
                for c, part in enumerate(join_entries(prod)):
                    abuf[u, tile_rows(c, m), lanes] = part
                model = join_entries(mat_mul_right_h(prod, second))
                sums = model if sums is None else [x + y for x, y in zip(sums, model)]
            for c in range(8):
                partial[it, u, c:c + 1, lanes] = jnp.sum(sums[c], axis=0, keepdims=True)

        for to in plane_next:
            part_copy(it, u, q, to).start()

    def backward_time(it, u):
        if it == 0:
            @pl.when(u != q)
            def _():
                vis_copy(u, q).wait_recv()
        model = partial[it, u]
        for src in plane_from:
            part_copy(it, u, src, q).wait_recv()
            model = model + part_in[it, u, src]
        res[u] = weight * (model - vis_all[u])
        for lo in range(0, N, 128):
            lanes = slice(lo, lo + 128)
            sky = sky_tiles(u, lanes)
            resid = split_entries([
                jnp.broadcast_to(res[u, c:c + 1, lanes], (ROWS, 128)) for c in range(8)])
            grads = [[None] * (8 * tiles), [None] * (8 * tiles)]
            for m in range(tiles):
                prod = split_entries([abuf[u, tile_rows(c, m), lanes] for c in range(8)])
                second = split_entries([gp[u, 1, tile_rows(c, m), lanes] for c in range(8)])
                first_grad = join_entries(mat_mul(resid, mat_mul_right_h(second, sky[m])))
                second_grad = join_entries(mat_mul_left_h(resid, prod))
                for c in range(8):
                    grads[0][c * tiles + m] = first_grad[c]
                    grads[1][c * tiles + m] = second_grad[c]
            for e in range(2):
                for pair in range(4 * tiles):
                    both = jnp.concatenate(grads[e][2 * pair:2 * pair + 2], axis=0)
                    high = both.astype(jnp.bfloat16)
                    low = (both - high.astype(jnp.float32)).astype(jnp.bfloat16)
                    here = slice(e * N + lo, e * N + lo + 128)
                    xbuf[u, 16 * pair:16 * pair + 16, here] = high
                    xbuf[u, 8 * D + 16 * pair:8 * D + 16 * pair + 16, here] = low

    def scatter_half(it, h):
        def add_time(u, total):
            return total + lax.dot_general(
                xbuf[u], oh[u, h * half:(h + 1) * half, :], (((1,), (1,)), ((), ())),
                preferred_element_type=jnp.float32)

        total = lax.fori_loop(0, Q, add_time, jnp.zeros((16 * D, half), jnp.float32))
        total = total[:8 * D] + total[8 * D:]
        for k in range(half // 128):
            acc[h, k] = total[:, k * 128:(k + 1) * 128]
        for v in range(Z):
            for d in range(nd):
                for k in range(half // 128):
                    gout[it, h, v, :, d * half + k * 128:d * half + (k + 1) * 128] = (
                        acc[h, k, pl.ds(v * nd + d, 8, stride=D), :])
        for v in column_others:
            go_copy(it, h, z, v).start()

    def consensus():
        sums = [jn[f] + du[f] / rho[...] for f in range(F)]
        for j in range(degrees):
            total = None
            for f in range(F):
                term = float(basis[f, j]) * sums[f]
                total = term if total is None else total + term
            poly_out[j] = total
        for f in range(F):
            total = None
            for j in range(degrees):
                term = float(basis[f, j]) * poly_out[j]
                total = term if total is None else total + term
            fit[f] = total

    for v in column_others:
        gz_copy(v, z).wait_recv()

    for it in range(ITERS):
        set_table()
        if it == 0:
            def gather_step(i, _):
                gather_time(i)
                return 0

            def forward_step(i, _):
                @pl.when(i != q)
                def _():
                    coh_copy(i, q).wait_recv()
                forward_time(it, i)
                return 0

            lax.fori_loop(0, Q, gather_step, 0)
            lax.fori_loop(0, Q, forward_step, 0)
            for f in freq_others:
                state_copy(0, f, fi).wait_recv()
                state_copy(1, f, fi).wait_recv()
            consensus()
        else:
            def both_step(i, _):
                gather_time(i)
                forward_time(it, i)
                return 0

            lax.fori_loop(0, Q, both_step, 0)

        def backward_step(i, _):
            backward_time(it, i)
            return 0

        lax.fori_loop(0, Q, backward_step, 0)

        for h in range(2):
            scatter_half(it, h)
        for h in range(2):
            grad = gout[it, h, z]
            for v in column_others:
                go_copy(it, h, v, z).wait_recv()
                grad = grad + gin[it, h, v]
            for d in range(nd):
                de[it, fi, :, d * S + h * half:d * S + (h + 1) * half] = grad[:, d * half:(d + 1) * half]
        descent = de[it, fi] + du[fi] + rho[...] * (jn[fi] - fit[fi])
        de[it, fi] = descent
        squares = descent * descent
        total = squares[:, 0:128]
        for lo in range(128, L, 128):
            total = total + squares[:, lo:lo + 128]
        sq[it, q] = total
        last = it + 1 == ITERS
        if not last:
            for v in column_others:
                zd_copy(it, z, v).start()
        for f in freq_others:
            de_copy(it, fi, f).start()
        for to in plane_next:
            sq_copy(it, to).start()
        sq_all(it).wait_recv()
        sqs[it, fi * Z + z] = jnp.sum(sq[it], axis=0)
        each_other(lambda f, v: sums_copy(it, f, v).start())
        sums_all(it).wait_recv()
        for f in freq_others:
            de_copy(it, f, fi).wait_recv()
        if it == 0:
            for f in freq_others:
                state_copy(0, fi, f).wait_send()
                state_copy(1, fi, f).wait_send()
            for v in column_others:
                gz_copy(z, v).wait_send()
        scales = []
        for f in range(F):
            tile = jnp.sum(sqs[it, pl.ds(f * Z, Z)], axis=0)
            whole = jnp.sum(jnp.sum(tile, axis=1, keepdims=True), axis=0, keepdims=True)
            scale = jnp.sqrt(whole / (8.0 * K * S) + epsilon)
            scales.append(scale)
            jn[f] = jn[f] - step_size * de[it, f] / scale
        consensus()
        for f in range(F):
            du[f] = du[f] + rho[...] * (jn[f] - fit[f])
        if not last:
            own = scales[0]
            for f in range(1, F):
                own = jnp.where(fi == f, scales[f], own)
            gz[z] = jn[fi]
            for v in column_others:
                zd_copy(it, v, z).wait_recv()
                gz[v] = gz[v] - step_size * zde[it, v] / own

    jones_out[...] = jn[fi]
    dual_out[...] = du[fi]
    for to in plane_next:
        st_copy(q, to).wait_send()
        vis_copy(q, to).wait_send()
        coh_copy(q, to).wait_send()
        for it in range(ITERS):
            for u in range(Q):
                part_copy(it, u, q, to).wait_send()
    for it in range(ITERS):
        for v in column_others:
            go_copy(it, 0, z, v).wait_send()
            go_copy(it, 1, z, v).wait_send()
            if it + 1 < ITERS:
                zd_copy(it, z, v).wait_send()
        sq_all(it).wait_send()
        sums_all(it).wait_send()
        for f in freq_others:
            de_copy(it, fi, f).wait_send()


def body(visibilities, coherency, stations, jones, dual, cluster, rho_table):
    T = lax.axis_size("tm")
    F = lax.axis_size("freq")
    K, N = coherency.shape[3], coherency.shape[4]
    L = jones.shape[2]
    nd = K // T
    S = L // nd
    Z = max(ROWS // nd, math.gcd(T, 4))
    Q = T // Z
    D = Z * nd
    basis = poly_basis(F, min(3, F - 1))
    degrees = basis.shape[1]
    weight = np.float32(math.sqrt(S / (2.0 * T * N)))
    vmem = pl.BlockSpec(memory_space=pltpu.VMEM)
    smem = pl.BlockSpec(memory_space=pltpu.SMEM)
    anywhere = pl.BlockSpec(memory_space=pltpu.HBM)
    f32, bf16 = jnp.float32, jnp.bfloat16
    dma = pltpu.SemaphoreType.DMA
    jones_out, dual_out, poly = pl.pallas_call(
        functools.partial(kernel, T, F, Z, nd, S, K, N, basis, weight),
        out_shape=(
            jax.ShapeDtypeStruct((8, L), f32),
            jax.ShapeDtypeStruct((8, L), f32),
            jax.ShapeDtypeStruct((degrees, 8, L), f32),
        ),
        in_specs=[anywhere] * 5 + [smem] * 2,
        out_specs=(vmem, vmem, vmem),
        scratch_shapes=[
            pltpu.VMEM((Q, 8, N), f32),
            pltpu.VMEM((8, K, N), bf16),
            pltpu.VMEM((Q, 8 * D, N), bf16),
            pltpu.VMEM((Q, 8 * D, N), bf16),
            pltpu.VMEM((Q, 2, N), jnp.int32),
            pltpu.VMEM((Q, S, 2 * N), bf16),
            pltpu.VMEM((16 * D, S), bf16),
            pltpu.VMEM((2, S // 128, 8 * D, 128), f32),
            pltpu.VMEM((Z, 8, L), f32),
            pltpu.VMEM((ITERS, Z, 8, L), f32),
            pltpu.VMEM((Q, 2, 8 * D, N), f32),
            pltpu.VMEM((Q, 8 * D, N), f32),
            pltpu.VMEM((Q, 16 * D, 2 * N), bf16),
            pltpu.VMEM((ITERS, Q, 8, N), f32),
            pltpu.VMEM((ITERS, Q, Q, 8, N), f32),
            pltpu.VMEM((Q, 8, N), f32),
            pltpu.VMEM((2, S // 256, 8 * D, 128), f32),
            pltpu.VMEM((ITERS, 2, Z, 8, L // 2), f32),
            pltpu.VMEM((ITERS, 2, Z, 8, L // 2), f32),
            pltpu.VMEM((F, 8, L), f32),
            pltpu.VMEM((F, 8, L), f32),
            pltpu.VMEM((ITERS, F, 8, L), f32),
            pltpu.VMEM((F, 8, L), f32),
            pltpu.VMEM((8, L), f32),
            pltpu.VMEM((ITERS, Q, 8, 128), f32),
            pltpu.VMEM((ITERS, F * Z, 8, 128), f32),
            dma((5,)), dma((Q,)), dma((Q,)), dma((Q,)), dma((Q,)), dma((Q,)), dma((Q,)), dma((Z,)), dma((Z,)),
            dma((ITERS, Z)), dma((ITERS, Z)), dma((ITERS, Q, Q)), dma((ITERS, Q, Q)),
            dma((ITERS, 2, Z)), dma((ITERS, 2, Z)),
            dma((2, F)), dma((2, F)), dma((ITERS, F)), dma((ITERS, F)), dma((ITERS,)), dma((ITERS,)), dma((ITERS,)), dma((ITERS,)),
        ],
        compiler_params=pltpu.CompilerParams(
            collective_id=0, has_side_effects=True, vmem_limit_bytes=60 * 1024 * 1024),
        cost_estimate=pl.CostEstimate(flops=10**10, bytes_accessed=10**7, transcendentals=0),
    )(visibilities[0, 0], coherency[0, 0], stations[0], jones[0], dual[0], cluster, rho_table)
    return jones_out[None], dual_out[None], poly


def solution(mesh):
    return jax.shard_map(
        body,
        mesh=mesh,
        in_specs=(
            P("tm", "freq", None, None),
            P("tm", "freq", None, None, None),
            P("tm", None, None),
            P("freq", None, "tm"),
            P("freq", None, "tm"),
            P(),
            P(),
        ),
        out_specs=(P("freq", None, "tm"), P("freq", None, "tm"), P(None, None, "tm")),
        check_vma=False,
    )
```

profile of v0, /device:TPU:0, one launch (start us, length us, event | category | flops | bytes accessed | tf_op | source)
XLA Modules:
  0.0 64.9 jit_solution(12429138546018650883)
XLA Ops:
  0.6 61.2 %shard_map.94 = (f32[8,2048]{1,0:T(8,128)}, f32[8,2048]{1,0:T(8,128)}, f32[1,8,2048]{2,1,0:T(8,128)}) custom-call(f32[8,512]{1,0:T(8,128)} %bitcast.12, bf16[8,64,512]{2,1,0:T(8,128)(2,1)} %bitcast.9, s32[2,512]{1,0:T(2,128)} %bitcast.13, f32[8,2048]{1,0:T(8,128)} %bitcast.10, f32[8,2048]{1,0:T(8,128)} %bitcast.11, s32[64]{0:T(128)} %cluster_ref.1, f32[8]{0:T(128)} %table_ref.1), custom_call_target="tpu_custom_call" | custom-call | flops 10000000000 | bytes 10000000 | tf_op jit(solution)/shard_map/pallas_call | solution.py:465
  61.9 0.0 copy-start.1
  61.9 1.5 %copy.13 = f32[1,8,2048]{2,1,0:T(8,128)} copy(f32[1,8,2048]{2,1,0:T(8,128)} %bitcast.8) | data formatting | bytes 131072
  63.4 0.0 copy-done.1
  63.4 0.0 copy-start
  63.4 0.6 copy.14
  64.0 0.2 copy-done
  64.3 0.6 copy.15
Async XLA Ops:
  61.9 1.5 %copy-start.1 = (f32[8,2048]{1,0:T(8,128)S(1)}, f32[8,2048]{1,0:T(8,128)}, u32[]{:S(2)}) copy-start(f32[8,2048]{1,0:T(8,128)} %get-tuple-element.7) | copy-start | bytes 196612
  63.4 0.9 %copy-start = (f32[1,8,2048]{2,1,0:T(8,128)S(1)}, f32[1,8,2048]{2,1,0:T(8,128)}, u32[]{:S(2)}) copy-start(f32[1,8,2048]{2,1,0:T(8,128)} %get-tuple-element.14) | copy-start | bytes 196612
where the time goes:
time: 65.1 us; the launch traced here: 64.9 us
  Pallas kernels  61.2 us (94%)
  local copies, waits for them, and re-layouts  3 us (5%)
    pallas_call x1, Pallas kernels, body(): pl.pallas_call(functools.partial(kernel, T, F, Z, nd, S, K, N, basis, wei...  61.2 us
    unnamed x7, local copies, waits for them, and re-layouts  3 us

commit v1 on v0

--- a/solution.py
+++ b/solution.py
@@ -65,7 +65,7 @@
     T, F, Z, nd, S, K, N, basis, weight,
     vis_hbm, coh_hbm, st_hbm, jones_hbm, dual_hbm, cluster_ref, table_ref,
     jones_out, dual_out, poly_out,
-    vis_all, coh_raw, coh_out, coh_in, st_all, oh, tab, tabs, gz, zde, gp, abuf, xbuf, partial, part_in, res, acc, gout, gin,
+    vis_all, coh_raw, coh_out, coh_in, st_all, oh, oht, tab, tabs, gz, zde, gp, abuf, xbuf, partial, part_in, res, acc, gout, gin,
     jn, du, de, fit, rho, sq, sqs,
     raw_sem, vi_ss, vi_rs, st_ss, st_rs, coh_ss, coh_rs, gz_ss, gz_rs, zd_ss, zd_rs, pa_ss, pa_rs, go_ss, go_rs,
     in_ss, in_rs, de_ss, de_rs, sq_ss, sq_rs, ss_ss, ss_rs,
@@ -103,7 +103,11 @@
 
     def part_copy(it, u, src, to):
         return remote(
-            partial.at[it, u], part_in.at[it, u, src], pa_ss.at[it, u, to], pa_rs.at[it, u, src], plane(to))
+            partial.at[it, u], part_in.at[it, u, src], pa_ss.at[it, u], pa_rs.at[it, u], plane(to))
+
+    def part_all(it, u):
+        span = part_in.at[it, u, pl.ds(0, Q - 1)]
+        return remote(span, span, pa_ss.at[it, u], pa_rs.at[it, u], plane(q))
 
     def gz_copy(src, to):
         return remote(gz.at[src], gz.at[src], gz_ss.at[to], gz_rs.at[src], column(to))
@@ -210,7 +214,13 @@
         @pl.when(u != q)
         def _():
             st_copy(u, q).wait_recv()
+        pair = jnp.concatenate([st_all[u]] * (ROWS // 2), axis=0).astype(jnp.float32)
+        turned = jnp.transpose(pair)
         for e in range(2):
+            for lo in range(0, N, 64):
+                ids = lax.broadcasted_iota(jnp.int32, (64, S), 1).astype(jnp.float32)
+                oht[u, e * N + lo:e * N + lo + 64, :] = jnp.where(
+                    ids == turned[lo:lo + 64, e:e + 1], 1.0, 0.0).astype(jnp.bfloat16)
             row = st_all[u, e:e + 1, :]
             for lo in range(0, S, 64):
                 ids = lax.broadcasted_iota(jnp.int32, (64, N), 0) + lo
@@ -271,8 +281,8 @@
             def _():
                 vis_copy(u, q).wait_recv()
         model = partial[it, u]
+        part_all(it, u).wait_recv()
         for src in plane_from:
-            part_copy(it, u, src, q).wait_recv()
             model = model + part_in[it, u, src]
         res[u] = weight * (model - vis_all[u])
         for lo in range(0, N, 128):
@@ -300,9 +310,8 @@
 
     def scatter_half(it, h):
         def add_time(u, total):
-            return total + lax.dot_general(
-                xbuf[u], oh[u, h * half:(h + 1) * half, :], (((1,), (1,)), ((), ())),
-                preferred_element_type=jnp.float32)
+            return total + jnp.dot(
+                xbuf[u], oht[u, :, h * half:(h + 1) * half], preferred_element_type=jnp.float32)
 
         total = lax.fori_loop(0, Q, add_time, jnp.zeros((16 * D, half), jnp.float32))
         total = total[:8 * D] + total[8 * D:]
@@ -429,15 +438,14 @@
         st_copy(q, to).wait_send()
         vis_copy(q, to).wait_send()
         coh_copy(q, to).wait_send()
-        for it in range(ITERS):
-            for u in range(Q):
-                part_copy(it, u, q, to).wait_send()
     for it in range(ITERS):
         for v in column_others:
             go_copy(it, 0, z, v).wait_send()
             go_copy(it, 1, z, v).wait_send()
             if it + 1 < ITERS:
                 zd_copy(it, z, v).wait_send()
+        for u in range(Q):
+            part_all(it, u).wait_send()
         sq_all(it).wait_send()
         sums_all(it).wait_send()
         for f in freq_others:
@@ -478,6 +486,7 @@
             pltpu.VMEM((Q, 8 * D, N), bf16),
             pltpu.VMEM((Q, 2, N), jnp.int32),
             pltpu.VMEM((Q, S, 2 * N), bf16),
+            pltpu.VMEM((Q, 2 * N, S), bf16),
             pltpu.VMEM((16 * D, S), bf16),
             pltpu.VMEM((2, S // 128, 8 * D, 128), f32),
             pltpu.VMEM((Z, 8, L), f32),
@@ -499,7 +508,7 @@
             pltpu.VMEM((ITERS, Q, 8, 128), f32),
             pltpu.VMEM((ITERS, F * Z, 8, 128), f32),
             dma((5,)), dma((Q,)), dma((Q,)), dma((Q,)), dma((Q,)), dma((Q,)), dma((Q,)), dma((Z,)), dma((Z,)),
-            dma((ITERS, Z)), dma((ITERS, Z)), dma((ITERS, Q, Q)), dma((ITERS, Q, Q)),
+            dma((ITERS, Z)), dma((ITERS, Z)), dma((ITERS, Q)), dma((ITERS, Q)),
             dma((ITERS, 2, Z)), dma((ITERS, 2, Z)),
             dma((2, F)), dma((2, F)), dma((ITERS, F)), dma((ITERS, F)), dma((ITERS,)), dma((ITERS,)), dma((ITERS,)), dma((ITERS,)),
         ],

time: 65.1 us -> 64.4 us (0.989)
  Pallas kernels: 61.2 us -> 60.5 us
    pallas_call x1, Pallas kernels: 61.2 us -> 60.5 us  [body(): pl.pallas_call(functools.partial(kernel, T, F, Z, nd, S, K, N, basis, wei...]
where the time goes in v1:
time: 64.4 us; the launch traced here: 64.2 us
  Pallas kernels  60.5 us (94%)
  local copies, waits for them, and re-layouts  3 us (5%)
  between operations  0.65 us (1%)
    pallas_call x1, Pallas kernels, body(): pl.pallas_call(functools.partial(kernel, T, F, Z, nd, S, K, N, basis, wei...  60.5 us
    unnamed x7, local copies, waits for them, and re-layouts  3 us

profile of v1, /device:TPU:0, one launch (start us, length us, event | category | flops | bytes accessed | tf_op | source)
XLA Modules:
  0.0 64.2 jit_solution(10553556148831025024)
XLA Ops:
  0.6 60.5 %shard_map.94 = (f32[8,2048]{1,0:T(8,128)}, f32[8,2048]{1,0:T(8,128)}, f32[1,8,2048]{2,1,0:T(8,128)}) custom-call(f32[8,512]{1,0:T(8,128)} %bitcast.12, bf16[8,64,512]{2,1,0:T(8,128)(2,1)} %bitcast.9, s32[2,512]{1,0:T(2,128)} %bitcast.13, f32[8,2048]{1,0:T(8,128)} %bitcast.10, f32[8,2048]{1,0:T(8,128)} %bitcast.11, s32[64]{0:T(128)} %cluster_ref.1, f32[8]{0:T(128)} %table_ref.1), custom_call_target="tpu_custom_call" | custom-call | flops 10000000000 | bytes 10000000 | tf_op jit(solution)/shard_map/pallas_call | solution.py:473
  61.2 0.0 copy-start.1
  61.2 1.5 %copy.13 = f32[1,8,2048]{2,1,0:T(8,128)} copy(f32[1,8,2048]{2,1,0:T(8,128)} %bitcast.8) | data formatting | bytes 131072
  62.7 0.0 copy-done.1
  62.7 0.0 copy-start
  62.7 0.6 copy.14
  63.3 0.2 copy-done
  63.6 0.6 copy.15
Async XLA Ops:
  61.2 1.5 %copy-start.1 = (f32[8,2048]{1,0:T(8,128)S(1)}, f32[8,2048]{1,0:T(8,128)}, u32[]{:S(2)}) copy-start(f32[8,2048]{1,0:T(8,128)} %get-tuple-element.7) | copy-start | bytes 196612
  62.7 0.9 %copy-start = (f32[1,8,2048]{2,1,0:T(8,128)S(1)}, f32[1,8,2048]{2,1,0:T(8,128)}, u32[]{:S(2)}) copy-start(f32[1,8,2048]{2,1,0:T(8,128)} %get-tuple-element.14) | copy-start | bytes 196612

commit v2 on v1

--- a/solution.py
+++ b/solution.py
@@ -64,9 +64,9 @@
 def kernel(
     T, F, Z, nd, S, K, N, basis, weight,
     vis_hbm, coh_hbm, st_hbm, jones_hbm, dual_hbm, cluster_ref, table_ref,
-    jones_out, dual_out, poly_out,
+    outs,
     vis_all, coh_raw, coh_out, coh_in, st_all, oh, oht, tab, tabs, gz, zde, gp, abuf, xbuf, partial, part_in, res, acc, gout, gin,
-    jn, du, de, fit, rho, sq, sqs,
+    jn, du, de, fit, rho, pol, sq, sqs,
     raw_sem, vi_ss, vi_rs, st_ss, st_rs, coh_ss, coh_rs, gz_ss, gz_rs, zd_ss, zd_rs, pa_ss, pa_rs, go_ss, go_rs,
     in_ss, in_rs, de_ss, de_rs, sq_ss, sq_rs, ss_ss, ss_rs,
 ):
@@ -325,18 +325,21 @@
         for v in column_others:
             go_copy(it, h, z, v).start()
 
-    def consensus():
+    def consensus(last=False):
         sums = [jn[f] + du[f] / rho[...] for f in range(F)]
         for j in range(degrees):
             total = None
             for f in range(F):
                 term = float(basis[f, j]) * sums[f]
+                if last and f == F - 1:
+                    outs[4 + 2 * j] = total
+                    outs[5 + 2 * j] = term
                 total = term if total is None else total + term
-            poly_out[j] = total
+            pol[j] = total
         for f in range(F):
             total = None
             for j in range(degrees):
-                term = float(basis[f, j]) * poly_out[j]
+                term = float(basis[f, j]) * pol[j]
                 total = term if total is None else total + term
             fit[f] = total
 
@@ -413,6 +416,9 @@
                 state_copy(1, fi, f).wait_send()
             for v in column_others:
                 gz_copy(z, v).wait_send()
+        if last:
+            outs[0] = jn[fi]
+            outs[2] = du[fi]
         scales = []
         for f in range(F):
             tile = jnp.sum(sqs[it, pl.ds(f * Z, Z)], axis=0)
@@ -420,20 +426,21 @@
             scale = jnp.sqrt(whole / (8.0 * K * S) + epsilon)
             scales.append(scale)
             jn[f] = jn[f] - step_size * de[it, f] / scale
-        consensus()
-        for f in range(F):
-            du[f] = du[f] + rho[...] * (jn[f] - fit[f])
-        if not last:
-            own = scales[0]
-            for f in range(1, F):
-                own = jnp.where(fi == f, scales[f], own)
+        consensus(last)
+        own = scales[0]
+        for f in range(1, F):
+            own = jnp.where(fi == f, scales[f], own)
+        if last:
+            outs[1] = step_size * de[it, fi] / own
+            outs[3] = rho[...] * (jn[fi] - fit[fi])
+        else:
+            for f in range(F):
+                du[f] = du[f] + rho[...] * (jn[f] - fit[f])
             gz[z] = jn[fi]
             for v in column_others:
                 zd_copy(it, v, z).wait_recv()
                 gz[v] = gz[v] - step_size * zde[it, v] / own
 
-    jones_out[...] = jn[fi]
-    dual_out[...] = du[fi]
     for to in plane_next:
         st_copy(q, to).wait_send()
         vis_copy(q, to).wait_send()
@@ -470,15 +477,11 @@
     anywhere = pl.BlockSpec(memory_space=pltpu.HBM)
     f32, bf16 = jnp.float32, jnp.bfloat16
     dma = pltpu.SemaphoreType.DMA
-    jones_out, dual_out, poly = pl.pallas_call(
+    outs = pl.pallas_call(
         functools.partial(kernel, T, F, Z, nd, S, K, N, basis, weight),
-        out_shape=(
-            jax.ShapeDtypeStruct((8, L), f32),
-            jax.ShapeDtypeStruct((8, L), f32),
-            jax.ShapeDtypeStruct((degrees, 8, L), f32),
-        ),
+        out_shape=jax.ShapeDtypeStruct((4 + 2 * degrees, 8, L), f32),
         in_specs=[anywhere] * 5 + [smem] * 2,
-        out_specs=(vmem, vmem, vmem),
+        out_specs=vmem,
         scratch_shapes=[
             pltpu.VMEM((Q, 8, N), f32),
             pltpu.VMEM((8, K, N), bf16),
@@ -505,6 +508,7 @@
             pltpu.VMEM((ITERS, F, 8, L), f32),
             pltpu.VMEM((F, 8, L), f32),
             pltpu.VMEM((8, L), f32),
+            pltpu.VMEM((degrees, 8, L), f32),
             pltpu.VMEM((ITERS, Q, 8, 128), f32),
             pltpu.VMEM((ITERS, F * Z, 8, 128), f32),
             dma((5,)), dma((Q,)), dma((Q,)), dma((Q,)), dma((Q,)), dma((Q,)), dma((Q,)), dma((Z,)), dma((Z,)),
@@ -516,7 +520,7 @@
             collective_id=0, has_side_effects=True, vmem_limit_bytes=60 * 1024 * 1024),
         cost_estimate=pl.CostEstimate(flops=10**10, bytes_accessed=10**7, transcendentals=0),
     )(visibilities[0, 0], coherency[0, 0], stations[0], jones[0], dual[0], cluster, rho_table)
-    return jones_out[None], dual_out[None], poly
+    return outs[0:1] - outs[1:2], outs[2:3] + outs[3:4], outs[4::2] + outs[5::2]
 
 
 def solution(mesh):

time: 64.4 us -> 63.1 us (0.980)
  local copies, waits for them, and re-layouts: 3 us -> 0 us
  other arithmetic: 0 us -> 1.68 us
    unnamed x7 -> x0, local copies, waits for them, and re-layouts: 3 us -> none
    add x0 -> x1, other arithmetic: none -> 1.68 us  [body(): outs[4::2] + outs[5::2]]
where the time goes in v2:
time: 63.1 us; the launch traced here: 62.9 us
  Pallas kernels  60.6 us (96%)
  other arithmetic  1.68 us (3%)
  between operations  0.64 us (1%)
    pallas_call x1, Pallas kernels, body(): pl.pallas_call(functools.partial(kernel, T, F, Z, nd, S, K, N, basis, wei...  60.6 us
    add x1, other arithmetic, body(): outs[4::2] + outs[5::2]  1.68 us

profile of v2, /device:TPU:0, one launch (start us, length us, event | category | flops | bytes accessed | tf_op | source)
XLA Modules:
  0.0 62.9 jit_solution(17464226180460175928)
XLA Ops:
  0.6 60.6 %shard_map.94 = f32[6,8,2048]{2,1,0:T(8,128)} custom-call(f32[8,512]{1,0:T(8,128)} %bitcast.8, bf16[8,64,512]{2,1,0:T(8,128)(2,1)} %bitcast.5, s32[2,512]{1,0:T(2,128)} %bitcast.9, f32[8,2048]{1,0:T(8,128)} %bitcast.6, f32[8,2048]{1,0:T(8,128)} %bitcast.7, s32[64]{0:T(128)} %cluster_ref.1, f32[8]{0:T(128)} %table_ref.1), custom_call_target="tpu_custom_call" | custom-call | flops 10000000000 | bytes 10000000 | tf_op jit(solution)/shard_map/pallas_call | solution.py:480
  61.2 1.7 %slice_add_fusion = (f32[1,8,2048]{2,1,0:T(8,128)}, f32[1,8,2048]{2,1,0:T(8,128)}, f32[1,8,2048]{2,1,0:T(8,128)}) fusion(f32[6,8,2048]{2,1,0:T(8,128)} %shard_map.94), kind=kLoop, calls=%fused_computation | loop fusion | flops 49152 | bytes 589824 | tf_op jit(solution)/shard_map/add | solution.py:523
